TPU v7x, 256 devices: a whole 4x4x8 slice. The times are simulated.
256 devices in a mesh: ctx: 128 (over z_hi, x, y, core), ch: 2 (over z_lo).
Axes of the slice: x: 4, y: 4, z: 8 (z_hi: 4, z_lo: 2; z = z_hi * 2 + z_lo), core: 2. Of those that a mesh axis runs over, the one named last changes fastest.
Arguments:
- activation: bfloat16 [16384, 256], P('ctx', 'ch'), may hold values from -1.5 to 1.5
- cotangent: bfloat16 [16384, 256], P('ctx', 'ch'), may hold values from -6 to 6
- filter_param: bfloat16 [16384, 16], P('ctx', 'ch'), may hold values from -6 to 6
- skip_gain: float32 [256], P('ch'), may hold values from 0.25 to 1.75
Outputs:
- input_grad: bfloat16 [16384, 256], P('ctx', 'ch')
- filter_grad: float32 [16384, 16], P('ctx', 'ch')
All inputs are finite; a program needn't handle non-finite values.
Results may differ from a plain program's by a relative error of at most 0.001.
Values may be sent and summed in bfloat16 or wider, within the bound.
No kernel may reach another device: no remote copies, remote signals or barrier semaphores. Data moves between devices by JAX's collectives and lax.ppermute only.
A program may use at most 64 MiB of HBM per device.

v0:
```python
import jax
import jax.numpy as jnp
from jax import lax
from jax.experimental import pallas as pl
from jax.experimental.pallas import tpu as pltpu
from jax.sharding import PartitionSpec as P

f32 = jnp.float32
bf16 = jnp.bfloat16
B = 128
R = 16
G = B // R


def pack_kernel(act_ref, cot_ref, filt_ref, out_ref, rows):
    here = lax.axis_index("ch")
    at = lax.broadcasted_iota(jnp.int32, (B, B), 0)
    to = lax.broadcasted_iota(jnp.int32, (B, B), 1)
    flip = jnp.where(at + to == B - 1, 1.0, 0.0).astype(bf16)
    cot_t = cot_ref[...].astype(f32).T
    rows[pl.ds(0, B, stride=4), :] = cot_t
    rows[pl.ds(2, B, stride=4), :] = cot_t
    rows[pl.ds(3, B, stride=4), :] = lax.dot_general(
        act_ref[...], flip, (((0,), (0,)), ((), ())), preferred_element_type=f32
    )
    filt = jnp.dot(filt_ref[...], flip, preferred_element_type=f32)
    for h in range(B // 8):
        mine = jnp.where(here == h % 2, filt, 0.0)
        rows[pl.ds(32 * h + 1, 8, stride=4), :] = mine
    out_ref[...] = rows[...].astype(bf16)


def correlate_kernel(in_ref, out_ref, rows, wide, hank, sums, spread):
    here = lax.axis_index("ch")
    rows[...] = in_ref[...].astype(f32)
    q_at = lax.broadcasted_iota(jnp.int32, (B, B), 0)
    b_at = lax.broadcasted_iota(jnp.int32, (B, B), 1)
    inside = b_at <= q_at
    filt = rows[pl.ds(1, B, stride=4), :] + rows[pl.ds(3, B, stride=4), :]
    results = []
    for half in range(2):
        weight = jnp.where(here == 1, rows[pl.ds(2 * half + 1, B, stride=4), :], filt).astype(bf16)
        padded = jnp.concatenate([jnp.zeros((B - R, B), bf16), weight], axis=0)
        for n in range(G):
            wide[:, n * B : (n + 1) * B] = padded[n * R : n * R + B]

        def turned(m):
            row = jnp.broadcast_to(rows[pl.ds(4 * m + 2 * half, 1), :], (B, B))
            return pltpu.roll(row, 1, 1, stride=1, stride_axis=0)

        after = jnp.zeros((B, B), f32)
        for m in reversed(range(B)):
            now = turned(m)
            block = jnp.where(inside, now, after).astype(bf16)
            hank[(m // R) * B : (m // R + 1) * B, (m % R) * B : (m % R + 1) * B] = block
            after = now
        sums[...] = jnp.dot(wide[...], hank[...], preferred_element_type=f32)
        spread[B * R :, :] = jnp.zeros((R * R, B), f32)
        for u in range(B):
            v, u0 = divmod(u, R)
            at = (G - 1 - v) * R
            spread[u * R : (u + 1) * R, :] = sums[at : at + R, u0 * B : (u0 + 1) * B]
        total = spread[pl.ds(0, B, stride=R), :]
        for r in range(1, R):
            total = total + spread[pl.ds((R + 1) * r, B, stride=R), :]
        results.append(total)
    both = results[0] + results[1]
    for half in range(2):
        out_ref[pl.ds(half, B, stride=2), :] = jnp.where(here == 1, both, results[half])


def finish_kernel(in_ref, cot_ref, gain_ref, grad_ref, filt_ref):
    here = lax.axis_index("ch")
    conv = in_ref[pl.ds(0, B, stride=2), :].T * (1.0 / B)
    grad_ref[...] = (gain_ref[...] * cot_ref[...].astype(f32) + conv).astype(bf16)
    totals = []
    for half in range(2):
        total = in_ref[pl.ds(16 * half + 1, 8, stride=2), :]
        for k in range(1, B // 16):
            total = total + in_ref[pl.ds(32 * k + 16 * half + 1, 8, stride=2), :]
        totals.append(total)
    filt_ref[...] = jnp.where(here == 1, totals[1], totals[0]) * (1.0 / B)


def on_device(activation, cotangent, filter_param, skip_gain):
    vmem = pl.BlockSpec(memory_space=pltpu.VMEM)
    axes = ("ctx", "ch")
    packed = pl.pallas_call(
        pack_kernel,
        out_shape=jax.ShapeDtypeStruct((4 * B, B), bf16),
        in_specs=[vmem] * 3,
        out_specs=vmem,
        scratch_shapes=[pltpu.VMEM((4 * B, B), f32)],
    )(activation, cotangent, filter_param.T)
    arrived = lax.all_to_all(packed.reshape(2 * B, 2, B), axes, 0, 0, tiled=True)
    partial = pl.pallas_call(
        correlate_kernel,
        out_shape=jax.ShapeDtypeStruct((2 * B, B), f32),
        in_specs=[vmem],
        out_specs=vmem,
        scratch_shapes=[
            pltpu.VMEM((4 * B, B), f32),
            pltpu.VMEM((B, G * B), bf16),
            pltpu.VMEM((G * B, R * B), bf16),
            pltpu.VMEM((B, R * B), f32),
            pltpu.VMEM((B * R + R * R, B), f32),
        ],
        compiler_params=pltpu.CompilerParams(vmem_limit_bytes=40 * 2**20),
    )(arrived.reshape(4 * B, B))
    back = lax.all_to_all(partial.reshape(2 * B, 1, B), axes, 0, 0, tiled=True)
    input_grad, filter_grad = pl.pallas_call(
        finish_kernel,
        out_shape=(jax.ShapeDtypeStruct((B, B), bf16), jax.ShapeDtypeStruct((8, B), f32)),
        in_specs=[vmem] * 3,
        out_specs=(vmem, vmem),
    )(back.reshape(2 * B, B), cotangent, skip_gain[None, :])
    return (input_grad, filter_grad.T)


def solution(mesh):
    return jax.shard_map(
        on_device,
        mesh=mesh,
        in_specs=(P("ctx", "ch"), P("ctx", "ch"), P("ctx", "ch"), P("ch")),
        out_specs=(P("ctx", "ch"), P("ctx", "ch")),
        check_vma=False,
    )
```

profile of v0, /device:TPU:1, one launch (start us, length us, event | category | flops | bytes accessed | tf_op | source)
XLA Modules:
  0.0 55.6 jit_solution(2652163824888670369)
XLA Ops:
  0.6 1.6 %shard_map.59 = bf16[512,128]{1,0:T(8,128)(2,1)} custom-call(bf16[128,128]{1,0:T(8,128)(2,1)} %act_ref.1, bf16[128,128]{1,0:T(8,128)(2,1)} %cot_ref.3, bf16[8,128]{1,0:T(8,128)(2,1)} %bitcast.13), custom_call_target="tpu_custom_call" | custom-call | tf_op jit(solution)/shard_map/pallas_call | solution.py:88
  2.3 28.4 %all_to_all.10 = bf16[256,2,128]{2,1,0:T(2,128)(2,1)S(1)} all-to-all(bf16[256,2,128]{2,1,0:T(2,128)(2,1)} %bitcast.12), channel_id=1, replica_groups=mesh['ctx'=128,'ch'=2] {'ctx','ch'}, dimensions={0} | all-to-all | bytes 262144 | tf_op jit(solution)/shard_map/all_to_all | solution.py:95
  30.7 4.0 %shard_map.60 = f32[256,128]{1,0:T(8,128)S(1)} custom-call(bf16[512,128]{1,0:T(8,128)(2,1)S(1)} %bitcast.9), custom_call_target="tpu_custom_call" | custom-call | tf_op jit(solution)/shard_map/pallas_call | solution.py:96
  34.7 19.3 %all_to_all.11 = f32[256,1,128]{2,1,0:T(1,128)} all-to-all(f32[256,1,128]{2,1,0:T(1,128)S(1)} %bitcast.10), channel_id=1, replica_groups=mesh['ctx'=128,'ch'=2] {'ctx','ch'}, dimensions={0} | all-to-all | bytes 262144 | tf_op jit(solution)/shard_map/all_to_all | solution.py:110
  53.9 1.6 %shard_map.61 = (bf16[128,128]{1,0:T(8,128)(2,1)}, f32[8,128]{1,0:T(8,128)}) custom-call(f32[256,128]{1,0:T(8,128)} %bitcast.11, bf16[128,128]{1,0:T(8,128)(2,1)} %cot_ref.3, f32[1,128]{1,0:T(1,128)} %bitcast.14), custom_call_target="tpu_custom_call" | custom-call | tf_op jit(solution)/shard_map/pallas_call | solution.py:111
where the time goes:
time: 55.8 us; the launch traced here: 55.6 us
  blocking collectives  47.7 us (85%)
  Pallas kernels  7.24 us (13%)
  between operations  0.64 us (1%)
    all_to_all x1, blocking collectives, on_device(): lax.all_to_all(packed.reshape(2 * B, 2, B), axes, 0, 0, tiled=True)  28.4 us
    all_to_all x1, blocking collectives, on_device(): back = lax.all_to_all(partial.reshape(2 * B, 1, B), axes, 0, 0, tiled=True)  19.3 us
    pallas_call x1, Pallas kernels, on_device(): pl.pallas_call(correlate_kernel, out_shape=jax.ShapeDtypeStruct((2 * B, B...  3.96 us
    pallas_call x1, Pallas kernels, on_device(): pl.pallas_call(finish_kernel, out_shape=(jax.ShapeDtypeStruct((B, B), bf1...  1.65 us
    pallas_call x1, Pallas kernels, on_device(): pl.pallas_call(pack_kernel, out_shape=jax.ShapeDtypeStruct((4 * B, B), bf...  1.63 us

commit v1 on v0

v1 whole, which is shorter than its diff:
```python
import jax
import jax.numpy as jnp
from jax import lax
from jax.experimental import pallas as pl
from jax.experimental.pallas import tpu as pltpu
from jax.sharding import PartitionSpec as P

f32 = jnp.float32
bf16 = jnp.bfloat16
B = 128
R = 16
G = B // R
Q = B // 2


def pack_kernel(act_hbm, cot_hbm, filt_hbm, out_ref, act_ref, cot_ref, filt_ref, rows, sems):
    pairs = ((cot_hbm, cot_ref), (act_hbm, act_ref), (filt_hbm, filt_ref))
    copies = [pltpu.make_async_copy(src, dst, sems.at[n]) for n, (src, dst) in enumerate(pairs)]
    for copy in copies:
        copy.start()
    here = lax.axis_index("ch")
    at = lax.broadcasted_iota(jnp.int32, (B, B), 0)
    to = lax.broadcasted_iota(jnp.int32, (B, B), 1)
    flip = jnp.where(at + to == B - 1, 1.0, 0.0).astype(bf16)
    copies[0].wait()
    cot_t = cot_ref[...].astype(f32).T
    rows[pl.ds(0, B, stride=4), :] = cot_t
    rows[pl.ds(2, B, stride=4), :] = cot_t
    copies[1].wait()
    rows[pl.ds(3, B, stride=4), :] = lax.dot_general(
        act_ref[...], flip, (((0,), (0,)), ((), ())), preferred_element_type=f32
    )
    copies[2].wait()
    filt = jnp.dot(filt_ref[...], flip, preferred_element_type=f32)
    for h in range(B // 8):
        mine = jnp.where(here == h % 2, filt, 0.0)
        rows[pl.ds(32 * h + 1, 8, stride=4), :] = mine
    out_ref[...] = rows[...].astype(bf16)


def correlate_kernel(in_ref, cot_hbm, gain_hbm, out_ref, direct_ref, rows, wide, hank, sums, cot_ref, gain_ref, sems):
    copies = [
        pltpu.make_async_copy(cot_hbm, cot_ref, sems.at[0]),
        pltpu.make_async_copy(gain_hbm, gain_ref, sems.at[1]),
    ]
    for copy in copies:
        copy.start()
    here = lax.axis_index("ch")
    rows[...] = in_ref[...].astype(f32)
    q_at = lax.broadcasted_iota(jnp.int32, (Q, B), 0)
    b_at = lax.broadcasted_iota(jnp.int32, (Q, B), 1)
    inside = b_at <= q_at + Q
    low = lax.broadcasted_iota(jnp.int32, (R, B), 1) < Q
    low8 = lax.broadcasted_iota(jnp.int32, (G, B), 1) < Q
    filt = rows[pl.ds(1, B, stride=4), :] + rows[pl.ds(3, B, stride=4), :]
    sums[:, :, B:, :] = jnp.zeros((2, R, R, B), f32)
    first = []
    for half in range(2):
        plain = jnp.where(here == 1, rows[pl.ds(2 * half + 1, B, stride=4), :], filt)
        moved = pltpu.roll(plain, Q, 1).astype(bf16)
        plain = plain.astype(bf16)
        zero = jnp.zeros((R, B), bf16)
        for v in range(G):
            for pair in range(G // 2):
                at = [(2 * pair + e - v) * R for e in range(2)]
                for k in range(2):
                    source = (moved, plain) if k == 0 else (plain, moved)
                    even, odd = (source[e][at[e] : at[e] + R] if at[e] >= 0 else zero for e in range(2))
                    wide[k * B + v * R : k * B + (v + 1) * R, pair * B : (pair + 1) * B] = jnp.where(low, even, odd)

        def turned(m):
            row = jnp.broadcast_to(rows[pl.ds(4 * m + 2 * half, 1), :], (Q, B))
            return pltpu.roll(row, Q + 1, 1, stride=1, stride_axis=0).astype(bf16)

        after = [turned(R * (n + 1)) for n in range(G - 1)] + [jnp.zeros((Q, B), bf16)]
        for u in reversed(range(R)):
            for n in range(G):
                now = turned(R * n + u)
                hank[n * Q : (n + 1) * Q, u * B : (u + 1) * B] = jnp.where(inside, now, after[n])
                after[n] = now
            if u % 2 == 0:
                cols = slice(u * B, (u + 2) * B)
                product = jnp.dot(wide[...], hank[:, cols], preferred_element_type=f32)
                for k in range(2):
                    for e in range(2):
                        sums[k, u + e, :B] = product[k * B : (k + 1) * B, e * B : (e + 1) * B]

        def total(k, u):
            found = None
            for r in range(R):
                carry, col = divmod(u + r, R)
                piece = sums[k, col, pl.ds(R * carry + r, G, stride=R), :]
                found = piece if found is None else found + piece
            return found

        ahead = pltpu.roll(total(1, R), Q, 1)
        for u in reversed(range(R)):
            now = pltpu.roll(total(1, u), Q, 1)
            result = total(0, u) + jnp.where(low8, now, ahead)
            ahead = now
            if half == 0:
                first.append(result)
            else:
                other = first[R - 1 - u]
                both = other + result
                out_ref[pl.ds(2 * u, G, stride=2 * R), :] = jnp.where(here == 1, both, other)
                out_ref[pl.ds(2 * u + 1, G, stride=2 * R), :] = jnp.where(here == 1, both, result)
    for copy in copies:
        copy.wait()
    direct_ref[...] = gain_ref[...] * cot_ref[...].astype(f32)


def finish_kernel(in_ref, direct_ref, grad_ref, filt_ref):
    here = lax.axis_index("ch")
    conv = in_ref[pl.ds(0, B, stride=2), :].T * (1.0 / B)
    grad_ref[...] = (direct_ref[...] + conv).astype(bf16)
    totals = []
    for half in range(2):
        total = in_ref[pl.ds(16 * half + 1, 8, stride=2), :]
        for k in range(1, B // 16):
            total = total + in_ref[pl.ds(32 * k + 16 * half + 1, 8, stride=2), :]
        totals.append(total)
    filt_ref[...] = jnp.where(here == 1, totals[1], totals[0]) * (1.0 / B)


def on_device(activation, cotangent, filter_param, skip_gain):
    vmem = pl.BlockSpec(memory_space=pltpu.VMEM)
    hbm = pl.BlockSpec(memory_space=pltpu.HBM)
    axes = ("ctx", "ch")
    activation, cotangent, filters, gain = (
        pltpu.with_memory_space_constraint(x, pltpu.HBM)
        for x in (activation, cotangent, filter_param.T, skip_gain[None, :])
    )
    packed = pl.pallas_call(
        pack_kernel,
        out_shape=jax.ShapeDtypeStruct((4 * B, B), bf16),
        in_specs=[hbm] * 3,
        out_specs=vmem,
        scratch_shapes=[
            pltpu.VMEM((B, B), bf16),
            pltpu.VMEM((B, B), bf16),
            pltpu.VMEM((8, B), bf16),
            pltpu.VMEM((4 * B, B), f32),
            pltpu.SemaphoreType.DMA((3,)),
        ],
        compiler_params=pltpu.CompilerParams(vmem_limit_bytes=8 * 2**20),
    )(activation, cotangent, filters)
    arrived = lax.all_to_all(packed.reshape(2 * B, 2, B), axes, 0, 0, tiled=True)
    partial, direct = pl.pallas_call(
        correlate_kernel,
        out_shape=(jax.ShapeDtypeStruct((2 * B, B), f32), jax.ShapeDtypeStruct((B, B), f32)),
        in_specs=[vmem, hbm, hbm],
        out_specs=(vmem, vmem),
        scratch_shapes=[
            pltpu.VMEM((4 * B, B), f32),
            pltpu.VMEM((2 * B, G * Q), bf16),
            pltpu.VMEM((G * Q, R * B), bf16),
            pltpu.VMEM((2, R, B + R, B), f32),
            pltpu.VMEM((B, B), bf16),
            pltpu.VMEM((1, B), f32),
            pltpu.SemaphoreType.DMA((2,)),
        ],
        compiler_params=pltpu.CompilerParams(vmem_limit_bytes=24 * 2**20),
    )(arrived.reshape(4 * B, B), cotangent, gain)
    back = lax.all_to_all(partial.reshape(2 * B, 1, B), axes, 0, 0, tiled=True)
    input_grad, filter_grad = pl.pallas_call(
        finish_kernel,
        out_shape=(jax.ShapeDtypeStruct((B, B), bf16), jax.ShapeDtypeStruct((8, B), f32)),
        in_specs=[vmem, vmem],
        out_specs=(vmem, vmem),
        compiler_params=pltpu.CompilerParams(vmem_limit_bytes=8 * 2**20),
    )(back.reshape(2 * B, B), direct)
    return (input_grad, filter_grad.T)


def solution(mesh):
    return jax.shard_map(
        on_device,
        mesh=mesh,
        in_specs=(P("ctx", "ch"), P("ctx", "ch"), P("ctx", "ch"), P("ch")),
        out_specs=(P("ctx", "ch"), P("ctx", "ch")),
        check_vma=False,
    )
```

time: 55.8 us -> 53.4 us (0.957)
  Pallas kernels: 7.24 us -> 5.63 us
  blocking collectives: 47.7 us -> 46.9 us
    pallas_call x1, Pallas kernels: 1.65 us -> 0.72 us  [on_device(): pl.pallas_call(finish_kernel, out_shape=(jax.ShapeDtypeStruct((B, B), bf1...]
    all_to_all x1, blocking collectives: 19.3 us -> 18.6 us  [on_device(): back = lax.all_to_all(partial.reshape(2 * B, 1, B), axes, 0, 0, tiled=True)]
where the time goes in v1:
time: 53.4 us; the launch traced here: 53.1 us
  blocking collectives  46.9 us (88%)
  Pallas kernels  5.63 us (11%)
  between operations  0.65 us (1%)
    all_to_all x1, blocking collectives, on_device(): lax.all_to_all(packed.reshape(2 * B, 2, B), axes, 0, 0, tiled=True)  28.2 us
    all_to_all x1, blocking collectives, on_device(): back = lax.all_to_all(partial.reshape(2 * B, 1, B), axes, 0, 0, tiled=True)  18.6 us
    pallas_call x1, Pallas kernels, on_device(): pl.pallas_call(correlate_kernel, out_shape=(jax.ShapeDtypeStruct((2 * B,...  3.69 us
    pallas_call x1, Pallas kernels, on_device(): pl.pallas_call(pack_kernel, out_shape=jax.ShapeDtypeStruct((4 * B, B), bf...  1.22 us

profile of v1, /device:TPU:1, one launch (start us, length us, event | category | flops | bytes accessed | tf_op | source)
XLA Modules:
  0.0 53.1 jit_solution(4096882873028139417)
XLA Ops:
  0.6 1.2 %shard_map.59 = bf16[512,128]{1,0:T(8,128)(2,1)S(1)} custom-call(bf16[128,128]{1,0:T(8,128)(2,1)} %act_hbm.1, bf16[128,128]{1,0:T(8,128)(2,1)} %cot_hbm.3, bf16[8,128]{1,0:T(8,128)(2,1)} %bitcast.13), custom_call_target="tpu_custom_call" | custom-call | tf_op jit(solution)/shard_map/pallas_call | solution.py:134
  1.9 28.2 %all_to_all.10 = bf16[256,2,128]{2,1,0:T(2,128)(2,1)S(1)} all-to-all(bf16[256,2,128]{2,1,0:T(2,128)(2,1)S(1)} %bitcast.11), channel_id=1, replica_groups=mesh['ctx'=128,'ch'=2] {'ctx','ch'}, dimensions={0} | all-to-all | bytes 262144 | tf_op jit(solution)/shard_map/all_to_all | solution.py:148
  30.1 3.7 %shard_map.60 = (f32[256,128]{1,0:T(8,128)S(1)}, f32[128,128]{1,0:T(8,128)S(1)}) custom-call(bf16[512,128]{1,0:T(8,128)(2,1)S(1)} %bitcast.9, bf16[128,128]{1,0:T(8,128)(2,1)} %cot_hbm.3, f32[1,128]{1,0:T(1,128)} %bitcast.14), custom_call_target="tpu_custom_call" | custom-call | tf_op jit(solution)/shard_map/pallas_call | solution.py:149
  33.8 18.6 %all_to_all.11 = f32[256,1,128]{2,1,0:T(1,128)S(1)} all-to-all(f32[256,1,128]{2,1,0:T(1,128)S(1)} %bitcast.12), channel_id=1, replica_groups=mesh['ctx'=128,'ch'=2] {'ctx','ch'}, dimensions={0} | all-to-all | bytes 262144 | tf_op jit(solution)/shard_map/all_to_all | solution.py:165
  52.4 0.7 %shard_map.61 = (bf16[128,128]{1,0:T(8,128)(2,1)}, f32[8,128]{1,0:T(8,128)}) custom-call(f32[256,128]{1,0:T(8,128)S(1)} %bitcast.10, f32[128,128]{1,0:T(8,128)S(1)} %get-tuple-element.7.direct_ref), custom_call_target="tpu_custom_call" | custom-call | tf_op jit(solution)/shard_map/pallas_call | solution.py:166

commit v2 on v0

v2 whole, which is shorter than its diff:
```python
import jax
import jax.numpy as jnp
from jax import lax
from jax.experimental import pallas as pl
from jax.experimental.pallas import tpu as pltpu
from jax.sharding import PartitionSpec as P

f32 = jnp.float32
bf16 = jnp.bfloat16
B = 128
R = 2
G = B // R
Q = 32
L = B // Q
E = 2 * L


def pack_kernel(
    act_hbm, cot_hbm, filt_hbm, gain_hbm, out_ref, direct_ref, act_ref, cot_ref, filt_ref, gain_ref, rows, sems
):
    pairs = ((cot_hbm, cot_ref), (act_hbm, act_ref), (filt_hbm, filt_ref), (gain_hbm, gain_ref))
    copies = [pltpu.make_async_copy(src, dst, sems.at[n]) for n, (src, dst) in enumerate(pairs)]
    for copy in copies:
        copy.start()
    here = lax.axis_index("ch")
    at = lax.broadcasted_iota(jnp.int32, (B, B), 0)
    to = lax.broadcasted_iota(jnp.int32, (B, B), 1)
    flip = jnp.where(at + to == B - 1, 1.0, 0.0).astype(bf16)
    copies[0].wait()
    cot = cot_ref[...].astype(f32)
    cot_t = cot.T
    rows[pl.ds(0, B, stride=4), :] = cot_t
    rows[pl.ds(2, B, stride=4), :] = cot_t
    copies[1].wait()
    rows[pl.ds(3, B, stride=4), :] = lax.dot_general(
        act_ref[...], flip, (((0,), (0,)), ((), ())), preferred_element_type=f32
    )
    copies[2].wait()
    filt = jnp.dot(filt_ref[...], flip, preferred_element_type=f32)
    for h in range(B // 8):
        mine = jnp.where(here == h % 2, filt, 0.0)
        rows[pl.ds(32 * h + 1, 8, stride=4), :] = mine
    out_ref[...] = rows[...].astype(bf16)
    copies[3].wait()
    direct_ref[...] = gain_ref[...] * cot


def correlate_kernel(in_ref, out_ref, rows, shifted, wide, hank, sums):
    here = lax.axis_index("ch")
    rows[...] = in_ref[...].astype(f32)
    q_at = lax.broadcasted_iota(jnp.int32, (Q, B), 0)
    b_at = lax.broadcasted_iota(jnp.int32, (Q, B), 1)
    inside = b_at <= q_at + B - Q
    to = lax.broadcasted_iota(jnp.int32, (B, B), 0)
    at = lax.broadcasted_iota(jnp.int32, (B, B), 1)
    swap = jnp.where(to + at - 2 * (to % 2) == B - 2, 1.0, 0.0).astype(bf16)
    group = at // Q
    lane = lax.broadcasted_iota(jnp.int32, (G, B), 1)
    filt = rows[pl.ds(1, B, stride=4), :] + rows[pl.ds(3, B, stride=4), :]
    shifted[:, B:, :] = jnp.zeros((L, 16, B), f32)
    sums[:, :, B:, :] = jnp.zeros((L, R, 8, B), f32)
    first = []
    for half in range(2):
        weight = jnp.where(here == 1, rows[pl.ds(2 * half + 1, B, stride=4), :], filt).astype(bf16)
        weight = jnp.dot(swap, weight, preferred_element_type=f32)
        for d in range(L):
            shifted[d, :B, :] = weight if d == 0 else pltpu.roll(weight, Q * d, 1)
        for k in range(L):
            for c in range(2):
                piece = None
                for j in range(L):
                    start = 2 * (E - 1) - 2 * L * c - 2 * j
                    taken = shifted[(j + k + 1) % L, start : start + B, :]
                    piece = taken if piece is None else jnp.where(group == j, taken, piece)
                piece = piece.astype(bf16)
                for i in range(B // 16):
                    wide[(L * i + k) * 16 : (L * i + k + 1) * 16, c * B : (c + 1) * B] = piece[16 * i : 16 * i + 16]

        def turned(m):
            row = jnp.broadcast_to(rows[pl.ds(4 * m + 2 * half, 1), :], (Q, B))
            return pltpu.roll(row, B - Q + 1, 1, stride=1, stride_axis=0).astype(bf16)

        after = jnp.zeros((Q, B), bf16)
        steps = G // E
        for e in reversed(range(steps)):
            slot = half * steps + e
            for m in reversed(range(R * E * e, R * E * (e + 1))):
                now = turned(m)
                n, u = divmod(m - R * E * e, R)
                hank[slot, n * Q : (n + 1) * Q, u * B : (u + 1) * B] = jnp.where(inside, now, after)
                after = now
            product = jnp.dot(wide[16 * L * (steps - 1 - e) :, :], hank[slot], preferred_element_type=f32)
            for i in range(e + 1):
                for k in range(L):
                    for u in range(R):
                        part = product[(L * i + k) * 16 : (L * i + k + 1) * 16, u * B : (u + 1) * B]
                        if e < steps - 1:
                            part = sums[k, u, 16 * i : 16 * i + 16, :] + part
                        sums[k, u, 16 * i : 16 * i + 16, :] = part

        def total(k, beta):
            found = None
            for r in range(R):
                carry, col = divmod(beta + r, R)
                piece = sums[k, col, pl.ds(R * carry + r, G, stride=R), :]
                found = piece if found is None else found + piece
            return found if k == 0 else pltpu.roll(found, B - Q * k, 1)

        results = [total(0, beta) for beta in range(R)]
        for k in range(1, L):
            turns = [total(k, beta) for beta in range(R + 1)]
            for beta in range(R):
                results[beta] = results[beta] + jnp.where(lane < B - Q * k, turns[beta], turns[beta + 1])
        if half == 0:
            first = results
            continue
        for beta in range(R):
            both = first[beta] + results[beta]
            for h, own in enumerate((first[beta], results[beta])):
                out_ref[pl.ds(2 * beta + h, G, stride=2 * R), :] = jnp.where(here == 1, both, own)


def finish_kernel(in_ref, direct_ref, grad_ref, filt_ref):
    here = lax.axis_index("ch")
    conv = in_ref[pl.ds(0, B, stride=2), :].T * (1.0 / B)
    grad_ref[...] = (direct_ref[...] + conv).astype(bf16)
    totals = []
    for half in range(2):
        total = in_ref[pl.ds(16 * half + 1, 8, stride=2), :]
        for k in range(1, B // 16):
            total = total + in_ref[pl.ds(32 * k + 16 * half + 1, 8, stride=2), :]
        totals.append(total)
    filt_ref[...] = jnp.where(here == 1, totals[1], totals[0]) * (1.0 / B)


def call_correlate(arrived):
    vmem = pl.BlockSpec(memory_space=pltpu.VMEM)
    return pl.pallas_call(
        correlate_kernel,
        out_shape=jax.ShapeDtypeStruct((2 * B, B), f32),
        in_specs=[vmem],
        out_specs=vmem,
        scratch_shapes=[
            pltpu.VMEM((4 * B, B), f32),
            pltpu.VMEM((L, B + 16, B), f32),
            pltpu.VMEM((L * B, E * Q), bf16),
            pltpu.VMEM((2 * G // E, E * Q, R * B), bf16),
            pltpu.VMEM((L, R, B + 8, B), f32),
        ],
        compiler_params=pltpu.CompilerParams(vmem_limit_bytes=24 * 2**20),
    )(arrived)


def on_device(activation, cotangent, filter_param, skip_gain):
    vmem = pl.BlockSpec(memory_space=pltpu.VMEM)
    hbm = pl.BlockSpec(memory_space=pltpu.HBM)
    axes = ("ctx", "ch")
    operands = (
        pltpu.with_memory_space_constraint(x, pltpu.HBM)
        for x in (activation, cotangent, filter_param.T, skip_gain[None, :])
    )
    packed, direct = pl.pallas_call(
        pack_kernel,
        out_shape=(jax.ShapeDtypeStruct((4 * B, B), bf16), jax.ShapeDtypeStruct((B, B), f32)),
        in_specs=[hbm] * 4,
        out_specs=(vmem, vmem),
        scratch_shapes=[
            pltpu.VMEM((B, B), bf16),
            pltpu.VMEM((B, B), bf16),
            pltpu.VMEM((8, B), bf16),
            pltpu.VMEM((1, B), f32),
            pltpu.VMEM((4 * B, B), f32),
            pltpu.SemaphoreType.DMA((4,)),
        ],
        compiler_params=pltpu.CompilerParams(vmem_limit_bytes=8 * 2**20),
    )(*operands)
    arrived = lax.all_to_all(packed.reshape(2 * B, 2, B), axes, 0, 0, tiled=True)
    partial = call_correlate(arrived.reshape(4 * B, B))
    back = lax.all_to_all(partial.reshape(2 * B, 1, B), axes, 0, 0, tiled=True)
    input_grad, filter_grad = pl.pallas_call(
        finish_kernel,
        out_shape=(jax.ShapeDtypeStruct((B, B), bf16), jax.ShapeDtypeStruct((8, B), f32)),
        in_specs=[vmem, vmem],
        out_specs=(vmem, vmem),
        compiler_params=pltpu.CompilerParams(vmem_limit_bytes=8 * 2**20),
    )(back.reshape(2 * B, B), direct)
    return (input_grad, filter_grad.T)


def solution(mesh):
    return jax.shard_map(
        on_device,
        mesh=mesh,
        in_specs=(P("ctx", "ch"), P("ctx", "ch"), P("ctx", "ch"), P("ch")),
        out_specs=(P("ctx", "ch"), P("ctx", "ch")),
        check_vma=False,
    )
```

time: 55.8 us -> 51.1 us (0.916)
  Pallas kernels: 7.24 us -> 3.34 us
  blocking collectives: 47.7 us -> 46.9 us
    pallas_call x2, Pallas kernels: 5.59 us -> 2.62 us  [the longest x1 1.38 us: call_correlate(): pl.pallas_call(correlate_kernel, out_shape=jax.ShapeDtypeStruct((2 * B, B...]
    pallas_call x1, Pallas kernels: 1.65 us -> 0.72 us  [on_device(): pl.pallas_call(finish_kernel, out_shape=(jax.ShapeDtypeStruct((B, B), bf1...]
    all_to_all x1, blocking collectives: 19.3 us -> 18.6 us  [on_device(): back = lax.all_to_all(partial.reshape(2 * B, 1, B), axes, 0, 0, tiled=True)]
where the time goes in v2:
time: 51.1 us; the launch traced here: 50.9 us
  blocking collectives  46.9 us (92%)
  Pallas kernels  3.34 us (7%)
  between operations  0.65 us (1%)
    all_to_all x1, blocking collectives, on_device(): lax.all_to_all(packed.reshape(2 * B, 2, B), axes, 0, 0, tiled=True)  28.2 us
    all_to_all x1, blocking collectives, on_device(): back = lax.all_to_all(partial.reshape(2 * B, 1, B), axes, 0, 0, tiled=True)  18.6 us
    pallas_call x1, Pallas kernels, call_correlate(): pl.pallas_call(correlate_kernel, out_shape=jax.ShapeDtypeStruct((2 * B, B...  1.38 us
    pallas_call x1, Pallas kernels, on_device(): pl.pallas_call(pack_kernel, out_shape=(jax.ShapeDtypeStruct((4 * B, B), b...  1.24 us

profile of v2, /device:TPU:1, one launch (start us, length us, event | category | flops | bytes accessed | tf_op | source)
XLA Modules:
  0.0 50.9 jit_solution(14211358793765277538)
XLA Ops:
  0.6 1.2 %shard_map.59 = (bf16[512,128]{1,0:T(8,128)(2,1)S(1)}, f32[128,128]{1,0:T(8,128)S(1)}) custom-call(bf16[128,128]{1,0:T(8,128)(2,1)} %act_hbm.1, bf16[128,128]{1,0:T(8,128)(2,1)} %cot_hbm.1, bf16[8,128]{1,0:T(8,128)(2,1)} %bitcast.13, f32[1,128]{1,0:T(1,128)} %bitcast.14), custom_call_target="tpu_custom_call" | custom-call | tf_op jit(solution)/shard_map/pallas_call | solution.py:162
  1.9 28.2 %all_to_all.10 = bf16[256,2,128]{2,1,0:T(2,128)(2,1)S(1)} all-to-all(bf16[256,2,128]{2,1,0:T(2,128)(2,1)S(1)} %bitcast.12), channel_id=1, replica_groups=mesh['ctx'=128,'ch'=2] {'ctx','ch'}, dimensions={0} | all-to-all | bytes 262144 | tf_op jit(solution)/shard_map/all_to_all | solution.py:177
  30.1 1.4 %shard_map.60 = f32[256,128]{1,0:T(8,128)S(1)} custom-call(bf16[512,128]{1,0:T(8,128)(2,1)S(1)} %bitcast.10), custom_call_target="tpu_custom_call" | custom-call | tf_op jit(solution)/shard_map/pallas_call | solution.py:138
  31.5 18.6 %all_to_all.11 = f32[256,1,128]{2,1,0:T(1,128)S(1)} all-to-all(f32[256,1,128]{2,1,0:T(1,128)S(1)} %bitcast.11), channel_id=1, replica_groups=mesh['ctx'=128,'ch'=2] {'ctx','ch'}, dimensions={0} | all-to-all | bytes 262144 | tf_op jit(solution)/shard_map/all_to_all | solution.py:179
  50.1 0.7 %shard_map.61 = (bf16[128,128]{1,0:T(8,128)(2,1)}, f32[8,128]{1,0:T(8,128)}) custom-call(f32[256,128]{1,0:T(8,128)S(1)} %bitcast.9, f32[128,128]{1,0:T(8,128)S(1)} %get-tuple-element.7.direct_ref), custom_call_target="tpu_custom_call" | custom-call | tf_op jit(solution)/shard_map/pallas_call | solution.py:180

commit v3 on v2

v3 whole, which is shorter than its diff:
```python
import jax
import jax.numpy as jnp
from jax import lax
from jax.experimental import pallas as pl
from jax.experimental.pallas import tpu as pltpu
from jax.sharding import PartitionSpec as P

f32 = jnp.float32
bf16 = jnp.bfloat16
B = 128
R = 2
G = B // R
Q = 32
L = B // Q
E = 2 * L


def pack_kernel(
    act_hbm, cot_hbm, filt_hbm, gain_hbm, out_ref, direct_ref, act_ref, cot_ref, filt_ref, gain_ref, rows, sems
):
    pairs = ((act_hbm, act_ref), (cot_hbm, cot_ref), (filt_hbm, filt_ref), (gain_hbm, gain_ref))
    copies = [pltpu.make_async_copy(src, dst, sems.at[n]) for n, (src, dst) in enumerate(pairs)]
    for copy in copies:
        copy.start()
    here = lax.axis_index("ch")
    at = lax.broadcasted_iota(jnp.int32, (B, B), 0)
    to = lax.broadcasted_iota(jnp.int32, (B, B), 1)
    flip = jnp.where(at + to == B - 1, 1.0, 0.0).astype(bf16)
    same = jnp.where(at == to, 1.0, 0.0).astype(bf16)
    for copy in copies:
        copy.wait()

    def turned(ref, onto):
        return lax.dot_general(ref[...], onto, (((0,), (0,)), ((), ())), preferred_element_type=f32)

    filt = jnp.dot(filt_ref[...], flip, preferred_element_type=f32)
    for h in range(B // 8):
        mine = jnp.where(here == h % 2, filt, 0.0)
        rows[pl.ds(32 * h + 1, 8, stride=4), :] = mine
    rows[pl.ds(3, B, stride=4), :] = turned(act_ref, flip)
    cot_t = turned(cot_ref, same)
    rows[pl.ds(0, B, stride=4), :] = cot_t
    rows[pl.ds(2, B, stride=4), :] = cot_t
    direct_ref[...] = gain_ref[...] * cot_ref[...].astype(f32)
    out_ref[...] = rows[...].astype(bf16)


def correlate_kernel(in_ref, out_ref, rows, shifted, wide, hank, sums):
    here = lax.axis_index("ch")
    rows[...] = in_ref[...].astype(f32)
    q_at = lax.broadcasted_iota(jnp.int32, (Q, B), 0)
    b_at = lax.broadcasted_iota(jnp.int32, (Q, B), 1)
    inside = b_at <= q_at + B - Q
    to = lax.broadcasted_iota(jnp.int32, (B, B), 0)
    at = lax.broadcasted_iota(jnp.int32, (B, B), 1)
    swap = jnp.where(to + at - 2 * (to % 2) == B - 2, 1.0, 0.0).astype(bf16)
    group = at // Q
    lane = lax.broadcasted_iota(jnp.int32, (G, B), 1)
    filt = rows[pl.ds(1, B, stride=4), :] + rows[pl.ds(3, B, stride=4), :]
    steps = G // E
    for half in range(2):
        shifted[half, :, B:, :] = jnp.zeros((L, 16, B), f32)
        sums[half, :, :, B:, :] = jnp.zeros((L, R, 8, B), f32)

    def prepare(half):
        weight = jnp.where(here == 1, rows[pl.ds(2 * half + 1, B, stride=4), :], filt).astype(bf16)
        weight = jnp.dot(swap, weight, preferred_element_type=f32)
        for d in range(L):
            shifted[half, d, :B, :] = weight if d == 0 else pltpu.roll(weight, Q * d, 1)
        for k in range(L):
            for c in range(2):
                piece = None
                for j in range(L):
                    start = 2 * (E - 1) - 2 * L * c - 2 * j
                    taken = shifted[half, (j + k + 1) % L, start : start + B, :]
                    piece = taken if piece is None else jnp.where(group == j, taken, piece)
                piece = piece.astype(bf16)
                for i in range(B // 16):
                    at_row = (L * i + k) * 16
                    wide[half, at_row : at_row + 16, c * B : (c + 1) * B] = piece[16 * i : 16 * i + 16]

    def turned(half, m):
        row = jnp.broadcast_to(rows[pl.ds(4 * m + 2 * half, 1), :], (Q, B))
        return pltpu.roll(row, B - Q + 1, 1, stride=1, stride_axis=0).astype(bf16)

    def spread(half, e, after):
        for m in reversed(range(R * E * e, R * E * (e + 1))):
            now = turned(half, m)
            n, u = divmod(m - R * E * e, R)
            hank[half, e, n * Q : (n + 1) * Q, u * B : (u + 1) * B] = jnp.where(inside, now, after)
            after = now
        return after

    def multiply(half, e):
        product = jnp.dot(wide[half, 16 * L * (steps - 1 - e) :, :], hank[half, e], preferred_element_type=f32)
        for i in range(e + 1):
            for k in range(L):
                for u in range(R):
                    part = product[(L * i + k) * 16 : (L * i + k + 1) * 16, u * B : (u + 1) * B]
                    if e < steps - 1:
                        part = sums[half, k, u, 16 * i : 16 * i + 16, :] + part
                    sums[half, k, u, 16 * i : 16 * i + 16, :] = part

    def total(half, k, beta):
        found = None
        for r in range(R):
            carry, col = divmod(beta + r, R)
            piece = sums[half, k, col, pl.ds(R * carry + r, G, stride=R), :]
            found = piece if found is None else found + piece
        return found if k == 0 else pltpu.roll(found, B - Q * k, 1)

    def combine(half):
        results = [total(half, 0, beta) for beta in range(R)]
        for k in range(1, L):
            turns = [total(half, k, beta) for beta in range(R + 1)]
            for beta in range(R):
                results[beta] = results[beta] + jnp.where(lane < B - Q * k, turns[beta], turns[beta + 1])
        return results

    prepare(0)
    prepare(1)
    after = [jnp.zeros((Q, B), bf16)] * 2
    for e in reversed(range(steps)):
        for half in range(2):
            after[half] = spread(half, e, after[half])
            multiply(half, e)
    found = [combine(half) for half in range(2)]
    for beta in range(R):
        both = found[0][beta] + found[1][beta]
        for h in range(2):
            out_ref[pl.ds(2 * beta + h, G, stride=2 * R), :] = jnp.where(here == 1, both, found[h][beta])


def finish_kernel(in_ref, direct_ref, grad_ref, filt_ref):
    here = lax.axis_index("ch")
    conv = in_ref[pl.ds(0, B, stride=2), :].T * (1.0 / B)
    grad_ref[...] = (direct_ref[...] + conv).astype(bf16)
    totals = []
    for half in range(2):
        total = in_ref[pl.ds(16 * half + 1, 8, stride=2), :]
        for k in range(1, B // 16):
            total = total + in_ref[pl.ds(32 * k + 16 * half + 1, 8, stride=2), :]
        totals.append(total)
    filt_ref[...] = jnp.where(here == 1, totals[1], totals[0]) * (1.0 / B)


def call_correlate(arrived):
    vmem = pl.BlockSpec(memory_space=pltpu.VMEM)
    return pl.pallas_call(
        correlate_kernel,
        out_shape=jax.ShapeDtypeStruct((2 * B, B), f32),
        in_specs=[vmem],
        out_specs=vmem,
        scratch_shapes=[
            pltpu.VMEM((4 * B, B), f32),
            pltpu.VMEM((2, L, B + 16, B), f32),
            pltpu.VMEM((2, L * B, E * Q), bf16),
            pltpu.VMEM((2, G // E, E * Q, R * B), bf16),
            pltpu.VMEM((2, L, R, B + 8, B), f32),
        ],
        compiler_params=pltpu.CompilerParams(vmem_limit_bytes=24 * 2**20),
    )(arrived)


def on_device(activation, cotangent, filter_param, skip_gain):
    vmem = pl.BlockSpec(memory_space=pltpu.VMEM)
    hbm = pl.BlockSpec(memory_space=pltpu.HBM)
    axes = ("ctx", "ch")
    operands = (
        pltpu.with_memory_space_constraint(x, pltpu.HBM)
        for x in (activation, cotangent, filter_param.T, skip_gain[None, :])
    )
    packed, direct = pl.pallas_call(
        pack_kernel,
        out_shape=(jax.ShapeDtypeStruct((4 * B, B), bf16), jax.ShapeDtypeStruct((B, B), f32)),
        in_specs=[hbm] * 4,
        out_specs=(vmem, vmem),
        scratch_shapes=[
            pltpu.VMEM((B, B), bf16),
            pltpu.VMEM((B, B), bf16),
            pltpu.VMEM((8, B), bf16),
            pltpu.VMEM((1, B), f32),
            pltpu.VMEM((4 * B, B), f32),
            pltpu.SemaphoreType.DMA((4,)),
        ],
        compiler_params=pltpu.CompilerParams(vmem_limit_bytes=8 * 2**20),
    )(*operands)
    arrived = lax.all_to_all(packed.reshape(2 * B, 2, B), axes, 0, 0, tiled=True)
    partial = call_correlate(arrived.reshape(4 * B, B))
    back = lax.all_to_all(partial.reshape(2 * B, 1, B), axes, 0, 0, tiled=True)
    input_grad, filter_grad = pl.pallas_call(
        finish_kernel,
        out_shape=(jax.ShapeDtypeStruct((B, B), bf16), jax.ShapeDtypeStruct((8, B), f32)),
        in_specs=[vmem, vmem],
        out_specs=(vmem, vmem),
        compiler_params=pltpu.CompilerParams(vmem_limit_bytes=8 * 2**20),
    )(back.reshape(2 * B, B), direct)
    return (input_grad, filter_grad.T)


def solution(mesh):
    return jax.shard_map(
        on_device,
        mesh=mesh,
        in_specs=(P("ctx", "ch"), P("ctx", "ch"), P("ctx", "ch"), P("ch")),
        out_specs=(P("ctx", "ch"), P("ctx", "ch")),
        check_vma=False,
    )
```

time: 51.1 us -> 50.8 us (level)
  no operation moved by 1% of the time
where the time goes in v3:
time: 50.8 us; the launch traced here: 50.6 us
  blocking collectives  46.9 us (92%)
  Pallas kernels  3.06 us (6%)
  between operations  0.65 us (1%)
    all_to_all x1, blocking collectives, on_device(): lax.all_to_all(packed.reshape(2 * B, 2, B), axes, 0, 0, tiled=True)  28.2 us
    all_to_all x1, blocking collectives, on_device(): back = lax.all_to_all(partial.reshape(2 * B, 1, B), axes, 0, 0, tiled=True)  18.6 us
    pallas_call x1, Pallas kernels, call_correlate(): pl.pallas_call(correlate_kernel, out_shape=jax.ShapeDtypeStruct((2 * B, B...  1.31 us
    pallas_call x1, Pallas kernels, on_device(): pl.pallas_call(pack_kernel, out_shape=(jax.ShapeDtypeStruct((4 * B, B), b...  1.03 us

profile of v3, /device:TPU:1, one launch (start us, length us, event | category | flops | bytes accessed | tf_op | source)
XLA Modules:
  0.0 50.6 jit_solution(8115372489339883604)
XLA Ops:
  0.6 1.0 %shard_map.59 = (bf16[512,128]{1,0:T(8,128)(2,1)S(1)}, f32[128,128]{1,0:T(8,128)S(1)}) custom-call(bf16[128,128]{1,0:T(8,128)(2,1)} %act_hbm.1, bf16[128,128]{1,0:T(8,128)(2,1)} %cot_hbm.1, bf16[8,128]{1,0:T(8,128)(2,1)} %bitcast.13, f32[1,128]{1,0:T(1,128)} %bitcast.14), custom_call_target="tpu_custom_call" | custom-call | tf_op jit(solution)/shard_map/pallas_call | solution.py:173
  1.7 28.2 %all_to_all.10 = bf16[256,2,128]{2,1,0:T(2,128)(2,1)S(1)} all-to-all(bf16[256,2,128]{2,1,0:T(2,128)(2,1)S(1)} %bitcast.12), channel_id=1, replica_groups=mesh['ctx'=128,'ch'=2] {'ctx','ch'}, dimensions={0} | all-to-all | bytes 262144 | tf_op jit(solution)/shard_map/all_to_all | solution.py:188
  29.9 1.3 %shard_map.60 = f32[256,128]{1,0:T(8,128)S(1)} custom-call(bf16[512,128]{1,0:T(8,128)(2,1)S(1)} %bitcast.10), custom_call_target="tpu_custom_call" | custom-call | tf_op jit(solution)/shard_map/pallas_call | solution.py:149
  31.2 18.6 %all_to_all.11 = f32[256,1,128]{2,1,0:T(1,128)S(1)} all-to-all(f32[256,1,128]{2,1,0:T(1,128)S(1)} %bitcast.11), channel_id=1, replica_groups=mesh['ctx'=128,'ch'=2] {'ctx','ch'}, dimensions={0} | all-to-all | bytes 262144 | tf_op jit(solution)/shard_map/all_to_all | solution.py:190
  49.9 0.7 %shard_map.61 = (bf16[128,128]{1,0:T(8,128)(2,1)}, f32[8,128]{1,0:T(8,128)}) custom-call(f32[256,128]{1,0:T(8,128)S(1)} %bitcast.9, f32[128,128]{1,0:T(8,128)S(1)} %get-tuple-element.7.direct_ref), custom_call_target="tpu_custom_call" | custom-call | tf_op jit(solution)/shard_map/pallas_call | solution.py:191

commit v4 on v3

--- a/solution.py
+++ b/solution.py
@@ -15,20 +15,12 @@
 E = 2 * L
 
 
-def pack_kernel(
-    act_hbm, cot_hbm, filt_hbm, gain_hbm, out_ref, direct_ref, act_ref, cot_ref, filt_ref, gain_ref, rows, sems
-):
-    pairs = ((act_hbm, act_ref), (cot_hbm, cot_ref), (filt_hbm, filt_ref), (gain_hbm, gain_ref))
-    copies = [pltpu.make_async_copy(src, dst, sems.at[n]) for n, (src, dst) in enumerate(pairs)]
-    for copy in copies:
-        copy.start()
+def pack_kernel(flip_ref, same_ref, act_ref, cot_ref, filt_ref, gain_ref, out_ref, direct_ref, rows):
     here = lax.axis_index("ch")
     at = lax.broadcasted_iota(jnp.int32, (B, B), 0)
     to = lax.broadcasted_iota(jnp.int32, (B, B), 1)
-    flip = jnp.where(at + to == B - 1, 1.0, 0.0).astype(bf16)
-    same = jnp.where(at == to, 1.0, 0.0).astype(bf16)
-    for copy in copies:
-        copy.wait()
+    flip = flip_ref[...]
+    same = same_ref[...]
 
     def turned(ref, onto):
         return lax.dot_general(ref[...], onto, (((0,), (0,)), ((), ())), preferred_element_type=f32)
@@ -55,7 +47,7 @@
     at = lax.broadcasted_iota(jnp.int32, (B, B), 1)
     swap = jnp.where(to + at - 2 * (to % 2) == B - 2, 1.0, 0.0).astype(bf16)
     group = at // Q
-    lane = lax.broadcasted_iota(jnp.int32, (G, B), 1)
+    lane = lax.broadcasted_iota(jnp.int32, (8, B), 1)
     filt = rows[pl.ds(1, B, stride=4), :] + rows[pl.ds(3, B, stride=4), :]
     steps = G // E
     for half in range(2):
@@ -101,21 +93,29 @@
                         part = sums[half, k, u, 16 * i : 16 * i + 16, :] + part
                     sums[half, k, u, 16 * i : 16 * i + 16, :] = part
 
-    def total(half, k, beta):
+    def total(half, e, k, beta):
         found = None
         for r in range(R):
             carry, col = divmod(beta + r, R)
-            piece = sums[half, k, col, pl.ds(R * carry + r, G, stride=R), :]
+            piece = sums[half, k, col, pl.ds(16 * e + R * carry + r, 8, stride=R), :]
             found = piece if found is None else found + piece
         return found if k == 0 else pltpu.roll(found, B - Q * k, 1)
 
-    def combine(half):
-        results = [total(half, 0, beta) for beta in range(R)]
+    def combine(half, e):
+        results = [total(half, e, 0, beta) for beta in range(R)]
         for k in range(1, L):
-            turns = [total(half, k, beta) for beta in range(R + 1)]
+            turns = [total(half, e, k, beta) for beta in range(R + 1)]
             for beta in range(R):
                 results[beta] = results[beta] + jnp.where(lane < B - Q * k, turns[beta], turns[beta + 1])
         return results
+
+    def finish(e):
+        found = [combine(half, e) for half in range(2)]
+        for beta in range(R):
+            both = found[0][beta] + found[1][beta]
+            for h in range(2):
+                at_row = 32 * e + 2 * beta + h
+                out_ref[pl.ds(at_row, 8, stride=2 * R), :] = jnp.where(here == 1, both, found[h][beta])
 
     prepare(0)
     prepare(1)
@@ -124,11 +124,8 @@
         for half in range(2):
             after[half] = spread(half, e, after[half])
             multiply(half, e)
-    found = [combine(half) for half in range(2)]
-    for beta in range(R):
-        both = found[0][beta] + found[1][beta]
-        for h in range(2):
-            out_ref[pl.ds(2 * beta + h, G, stride=2 * R), :] = jnp.where(here == 1, both, found[h][beta])
+    for e in reversed(range(steps)):
+        finish(e)
 
 
 def finish_kernel(in_ref, direct_ref, grad_ref, filt_ref):
@@ -164,24 +161,19 @@
 
 def on_device(activation, cotangent, filter_param, skip_gain):
     vmem = pl.BlockSpec(memory_space=pltpu.VMEM)
-    hbm = pl.BlockSpec(memory_space=pltpu.HBM)
     axes = ("ctx", "ch")
-    operands = (
-        pltpu.with_memory_space_constraint(x, pltpu.HBM)
-        for x in (activation, cotangent, filter_param.T, skip_gain[None, :])
-    )
+    at = lax.broadcasted_iota(jnp.int32, (B, B), 0)
+    to = lax.broadcasted_iota(jnp.int32, (B, B), 1)
+    flip = jnp.where(at + to == B - 1, 1.0, 0.0).astype(bf16)
+    same = jnp.where(at == to, 1.0, 0.0).astype(bf16)
+    operands = (flip, same, activation, cotangent, filter_param.T, skip_gain[None, :])
     packed, direct = pl.pallas_call(
         pack_kernel,
         out_shape=(jax.ShapeDtypeStruct((4 * B, B), bf16), jax.ShapeDtypeStruct((B, B), f32)),
-        in_specs=[hbm] * 4,
+        in_specs=[vmem] * 6,
         out_specs=(vmem, vmem),
         scratch_shapes=[
-            pltpu.VMEM((B, B), bf16),
-            pltpu.VMEM((B, B), bf16),
-            pltpu.VMEM((8, B), bf16),
-            pltpu.VMEM((1, B), f32),
             pltpu.VMEM((4 * B, B), f32),
-            pltpu.SemaphoreType.DMA((4,)),
         ],
         compiler_params=pltpu.CompilerParams(vmem_limit_bytes=8 * 2**20),
     )(*operands)

time: 50.8 us -> 50.7 us (level)
  Pallas kernels: 3.06 us -> 2.22 us
  local copies, waits for them, and re-layouts: 0 us -> 0.72 us
    pallas_call x1, Pallas kernels: 1.03 us -> 0.21 us  [on_device(): pl.pallas_call(pack_kernel, out_shape=(jax.ShapeDtypeStruct((4 * B, B), b...]
    unnamed x0 -> x8, local copies, waits for them, and re-layouts: none -> 0.72 us
where the time goes in v4:
time: 50.7 us; the launch traced here: 50.5 us
  blocking collectives  46.9 us (93%)
  Pallas kernels  2.22 us (4%)
  local copies, waits for them, and re-layouts  0.72 us (1%)
  between operations  0.68 us (1%)
    all_to_all x1, blocking collectives, on_device(): lax.all_to_all(packed.reshape(2 * B, 2, B), axes, 0, 0, tiled=True)  28.2 us
    all_to_all x1, blocking collectives, on_device(): back = lax.all_to_all(partial.reshape(2 * B, 1, B), axes, 0, 0, tiled=True)  18.6 us
    pallas_call x1, Pallas kernels, call_correlate(): pl.pallas_call(correlate_kernel, out_shape=jax.ShapeDtypeStruct((2 * B, B...  1.29 us

profile of v4, /device:TPU:1, one launch (start us, length us, event | category | flops | bytes accessed | tf_op | source)
XLA Modules:
  0.0 50.5 jit_solution(17425051856490999085)
XLA Ops:
  0.6 0.0 copy-start.1
  0.6 0.0 copy-start
  0.7 0.0 copy-start.2
  0.7 0.0 copy-start.3
  0.7 0.7 %copy-done.1 = bf16[128,128]{1,0:T(8,128)(2,1)S(1)} copy-done((bf16[128,128]{1,0:T(8,128)(2,1)S(1)}, bf16[128,128]{1,0:T(8,128)(2,1)}, u32[]{:S(2)}) %copy-start.1) | copy-done | bytes 32792
  1.4 0.0 copy-done
  1.4 0.0 copy-done.2
  1.4 0.0 copy-done.3
  1.4 0.2 shard_map.59
  1.6 28.2 %all_to_all.10 = bf16[256,2,128]{2,1,0:T(2,128)(2,1)S(1)} all-to-all(bf16[256,2,128]{2,1,0:T(2,128)(2,1)S(1)} %bitcast.12), channel_id=1, replica_groups=mesh['ctx'=128,'ch'=2] {'ctx','ch'}, dimensions={0} | all-to-all | bytes 262144 | tf_op jit(solution)/shard_map/all_to_all | solution.py:180
  29.9 1.3 %shard_map.60 = f32[256,128]{1,0:T(8,128)S(1)} custom-call(bf16[512,128]{1,0:T(8,128)(2,1)S(1)} %bitcast.10), custom_call_target="tpu_custom_call" | custom-call | tf_op jit(solution)/shard_map/pallas_call | solution.py:146
  31.2 18.6 %all_to_all.11 = f32[256,1,128]{2,1,0:T(1,128)S(1)} all-to-all(f32[256,1,128]{2,1,0:T(1,128)S(1)} %bitcast.11), channel_id=1, replica_groups=mesh['ctx'=128,'ch'=2] {'ctx','ch'}, dimensions={0} | all-to-all | bytes 262144 | tf_op jit(solution)/shard_map/all_to_all | solution.py:182
  49.8 0.7 %shard_map.61 = (bf16[128,128]{1,0:T(8,128)(2,1)}, f32[8,128]{1,0:T(8,128)}) custom-call(f32[256,128]{1,0:T(8,128)S(1)} %bitcast.9, f32[128,128]{1,0:T(8,128)S(1)} %get-tuple-element.7.direct_ref), custom_call_target="tpu_custom_call" | custom-call | tf_op jit(solution)/shard_map/pallas_call | solution.py:183
  (1 shorter events, 0.0 us)
Async XLA Ops:
  0.6 0.8 %copy-start.1 = (bf16[128,128]{1,0:T(8,128)(2,1)S(1)}, bf16[128,128]{1,0:T(8,128)(2,1)}, u32[]{:S(2)}) copy-start(bf16[128,128]{1,0:T(8,128)(2,1)} %cot_ref.1) | copy-start | bytes 98308
  0.6 0.8 %copy-start = (bf16[128,128]{1,0:T(8,128)(2,1)S(1)}, bf16[128,128]{1,0:T(8,128)(2,1)}, u32[]{:S(2)}) copy-start(bf16[128,128]{1,0:T(8,128)(2,1)} %act_ref.1) | copy-start | bytes 98308
  0.7 0.7 %copy-start.2 = (bf16[128,8]{0,1:T(8,128)(2,1)S(1)}, bf16[128,8]{0,1:T(8,128)(2,1)}, u32[]{:S(2)}) copy-start(bf16[128,8]{0,1:T(8,128)(2,1)} %param.6) | copy-start | bytes 6148
  0.7 0.7 %copy-start.3 = (f32[128]{0:T(128)S(1)}, f32[128]{0:T(128)}, u32[]{:S(2)}) copy-start(f32[128]{0:T(128)} %param.7) | copy-start | bytes 1540
